TPU v7x, 512 devices: a whole 4x4x16 slice. The times are simulated.
512 devices in a mesh: expert: 32 (over x_lo, z), tensor: 16 (over y, x_hi, core).
Axes of the slice: x: 4 (x_hi: 2, x_lo: 2; x = x_hi * 2 + x_lo), y: 4, z: 16, core: 2. Of those that a mesh axis runs over, the one named last changes fastest.
Arguments:
- tokens: bfloat16 [1536, 5120], P('expert', 'tensor'), may hold values from -6 to 6
- expert_ids: int32 [1536, 6], P('expert'), may hold values from 0 to 31, all different within a row; in each aligned block of 48 rows (0 to 47, 48 to 95, ...) at most 18 rows name the same one
- route_weights: float32 [1536, 6], P('expert'), may hold values from 0.05 to 0.6
- routed_gate: bfloat16 [32, 1536, 5120], P('expert', 'tensor'), may hold values from -0.078125 to 0.078125
- routed_up: bfloat16 [32, 1536, 5120], P('expert', 'tensor'), may hold values from -0.078125 to 0.078125
- routed_down: bfloat16 [32, 1536, 5120], P('expert', None, 'tensor'), may hold values from -0.15625 to 0.15625
- shared_gate: bfloat16 [5120, 3072], P('expert', 'tensor'), may hold values from -0.078125 to 0.078125
- shared_up: bfloat16 [5120, 3072], P('expert', 'tensor'), may hold values from -0.078125 to 0.078125
- shared_down: bfloat16 [3072, 5120], P('tensor', 'expert'), may hold values from -0.21875 to 0.21875
- norm_gain: float32 [5120], replicated, may hold values from 0.25 to 1.75
- proj_weight: bfloat16 [2112, 5120], P('tensor'), may hold values from -0.078125 to 0.078125
Outputs:
- stream: bfloat16 [1536, 5120], P('expert', 'tensor')
- projected: bfloat16 [1536, 2112], P('expert', 'tensor')
Inputs may be any that keep to these rules, and one draw needn't show every extreme that they name: `expert_ids`: in each aligned block of 48 tokens (those of one index of expert) no expert is chosen by more than 18 tokens, and some expert is chosen by exactly 18; a token's 6 experts differ.
All inputs are finite; a program needn't handle non-finite values.
Results may differ from a plain program's by a relative error of at most 0.019.
Values may be sent and summed in bfloat16 or wider, within the bound.
No kernel may reach another device: no remote copies, remote signals or barrier semaphores. Data moves between devices by JAX's collectives and lax.ppermute only.
A program may use at most 128 MiB of HBM per device.

v0:
```python
import jax
import jax.numpy as jnp
from jax import lax
from jax.sharding import PartitionSpec as P


def swiglu(gate, up):
    return (jax.nn.silu(gate) * up).astype(jnp.bfloat16)


def dot_rows(left, right):
    return lax.dot_general(
        left, right, (((1,), (1,)), ((), ())), preferred_element_type=jnp.float32
    )


def per_device(
    tokens,
    expert_ids,
    route_weights,
    routed_gate,
    routed_up,
    routed_down,
    shared_gate,
    shared_up,
    shared_down,
    norm_gain,
    proj_weight,
):
    tok_rows = tokens.shape[0]
    local_width = tokens.shape[1]
    top = expert_ids.shape[1]
    experts = lax.axis_size("expert")
    capacity = min(tok_rows, 2 * tok_rows * top // experts)
    features = lax.all_gather(tokens, "tensor", axis=1, tiled=True)
    flat_ids = expert_ids.reshape(-1)
    onehot = (flat_ids[:, None] == jnp.arange(experts, dtype=jnp.int32)[None, :]).astype(jnp.int32)
    slots = jnp.sum((jnp.cumsum(onehot, axis=0) - onehot) * onehot, axis=1)
    target = flat_ids * capacity + slots
    owners = jnp.repeat(jnp.arange(tok_rows, dtype=jnp.int32), top)
    sources = jnp.full((experts * capacity,), tok_rows, jnp.int32).at[target].set(owners)
    gate_w = routed_gate[0]
    up_w = routed_up[0]
    down_w = routed_down[0]
    padded = jnp.concatenate([features, jnp.zeros((1, features.shape[1]), features.dtype)], axis=0)
    outgoing = padded[sources].reshape(experts, capacity, features.shape[1])
    arrived = lax.all_to_all(outgoing, "expert", split_axis=0, concat_axis=0, tiled=True)
    count = arrived.shape[1]
    rows = arrived.reshape(-1, arrived.shape[2])
    hidden = swiglu(dot_rows(rows, gate_w), dot_rows(rows, up_w))
    hidden_all = lax.all_gather(hidden, "tensor", axis=1, tiled=True)
    result = jnp.dot(hidden_all, down_w, preferred_element_type=jnp.float32).astype(jnp.bfloat16)
    result = result.reshape(experts, count, result.shape[1])
    returned = lax.all_to_all(result, "expert", split_axis=0, concat_axis=0, tiled=True)
    flat_back = returned.reshape(experts * capacity, returned.shape[2])
    picked = flat_back[target].reshape(tok_rows, top, returned.shape[2]).astype(jnp.float32)
    routed = jnp.sum(picked * route_weights[:, :, None], axis=1)
    gate_sum = jnp.dot(
        features,
        lax.all_gather(shared_gate, "expert", axis=0, tiled=True),
        preferred_element_type=jnp.float32,
    )
    up_sum = jnp.dot(
        features,
        lax.all_gather(shared_up, "expert", axis=0, tiled=True),
        preferred_element_type=jnp.float32,
    )
    shared_hidden = swiglu(gate_sum, up_sum)
    shared_terms = jnp.dot(
        shared_hidden,
        lax.all_gather(shared_down, "expert", axis=1, tiled=True),
        preferred_element_type=jnp.float32,
    )
    rank = lax.axis_index("tensor")
    shared_full = lax.psum(shared_terms.astype(jnp.bfloat16), "tensor").astype(jnp.float32)
    shared_mine = lax.dynamic_slice_in_dim(shared_full, rank * local_width, local_width, 1)
    stream = (tokens.astype(jnp.float32) + shared_mine + routed).astype(jnp.bfloat16)
    stream_all = lax.all_gather(stream, "tensor", axis=1, tiled=True)
    values = stream_all.astype(jnp.float32)
    scale = lax.rsqrt(jnp.mean(values * values, axis=1, keepdims=True) + 1e-06)
    normed = (values * scale * norm_gain[None, :]).astype(jnp.bfloat16)
    projected = dot_rows(normed, proj_weight).astype(jnp.bfloat16)
    return (stream, projected)


def solution(mesh):
    in_specs = (
        P("expert", "tensor"),
        P("expert", None),
        P("expert", None),
        P("expert", "tensor", None),
        P("expert", "tensor", None),
        P("expert", None, "tensor"),
        P("expert", "tensor"),
        P("expert", "tensor"),
        P("tensor", "expert"),
        P(),
        P("tensor", None),
    )
    out_specs = (P("expert", "tensor"), P("expert", "tensor"))
    return jax.shard_map(
        per_device, mesh=mesh, in_specs=in_specs, out_specs=out_specs, check_vma=False
    )
```

profile of v0, /device:TPU:1, one launch (start us, length us, event | category | flops | bytes accessed | tf_op | source)
XLA Modules:
  0.0 1078.2 jit_solution(14754052590517255412)
XLA Ops:
  7.2 0.0 copy-start
  7.2 0.0 all-gather.13.cloned.1.call-start
  7.2 0.9 copy.26
  8.1 0.7 broadcast_multiply_fusion
  8.8 0.1 eq.22
  8.9 0.9 reduce-window.6
  9.8 0.2 slice_reduce_fusion
  10.1 0.1 bitcast_bitcast_fusion
  10.2 0.1 copy.25
  10.3 0.1 mul.68
  10.4 0.1 reshape.102
  10.6 2.9 scatter_custom_fusion
  13.5 29.4 %all-gather = bf16[16,320,48]{1,2,0:T(8,128)(2,1)S(1)} all-gather(bf16[1,320,48]{1,2,0:T(8,128)(2,1)} %bitcast.43), channel_id=1, replica_groups=mesh['expert'=32,'tensor'=16] {'tensor'}, dimensions={0}, use_global_device_ids=true | all-gather | bytes 522240 | tf_op jit(solution)/shard_map/all_gather | solution.py:35
  43.0 0.1 copy.24
  43.1 0.4 reshape.108
  43.6 6.0 gather_fusion
  49.6 8.5 reshape.76
  58.1 359.3 %all_to_all.10 = bf16[32,18,5120]{2,1,0:T(8,128)(2,1)} all-to-all(bf16[32,18,5120]{2,1,0:T(8,128)(2,1)} %reshape.76), channel_id=1, replica_groups=mesh['expert'=32,'tensor'=16] {'expert'}, dimensions={0} | all-to-all | bytes 11796480 | tf_op jit(solution)/shard_map/all_to_all | solution.py:47
  417.4 0.0 copy-start.2
  417.4 8.8 reshape.77
  426.2 0.0 copy-done.2
  426.2 0.0 copy-start.1
  426.2 4.8 fusion.4
  431.0 0.0 copy-done.1
  431.0 0.0 copy-done.6
  431.1 2.6 fusion
  433.7 0.0 all-gather.13.cloned.1.call-update
  433.7 0.0 all-gather.7.cloned.1.call-start
  433.8 0.7 all-gather.7.cloned.1.call-update
  434.5 0.0 all-gather.11.cloned.1.call-start
  434.5 0.7 all-gather.11.cloned.1.call-update
  435.2 0.0 all-gather.9.cloned.1.call-start
  435.3 0.5 all-gather.9.cloned.1.call-update
  435.8 51.4 %all-gather.13.cloned.1.call-done = bf16[576,1536]{0,1:T(8,128)(2,1)} async-done(((bf16[576,96]{0,1:T(8,128)(2,1)}), bf16[576,1536]{0,1:T(8,128)(2,1)}) %all-gather.13.cloned.1.call-update) | async-done | bytes 1769488 | tf_op jit(solution)/shard_map/all_gather | solution.py:51
  487.2 2.8 convolution_convert_fusion.1
  490.0 0.2 copy.29
  490.2 1.0 reshape.78
  491.3 12.3 %all-to-all-start.1 = ((bf16[32,18,320]{2,1,0:T(8,128)(2,1)}), bf16[32,18,320]{2,1,0:T(8,128)(2,1)S(1)}, u32[]{:S(2)}, u32[]{:S(2)}) async-start(bf16[32,18,320]{2,1,0:T(8,128)(2,1)} %reshape.78), calls=%async_computation.1 | async-start | bytes 1179648 | tf_op jit(solution)/shard_map/all_to_all | solution.py:54
  503.6 0.2 all-reduce.4.cloned.1.call-start
  503.8 110.9 %all-gather.7.cloned.1.call-done = bf16[5120,192]{1,0:T(8,128)(2,1)} async-done(((bf16[160,192]{1,0:T(8,128)(2,1)}), bf16[5120,192]{1,0:T(8,128)(2,1)}) %all-gather.7.cloned.1.call-update) | async-done | bytes 1966096 | tf_op jit(solution)/shard_map/all_gather | solution.py:60
  614.7 2.3 fusion.20
  617.0 0.0 copy-start.5
  617.0 123.6 %all-gather.11.cloned.1.call-done = bf16[192,5120]{0,1:T(8,128)(2,1)} async-done(((bf16[192,160]{0,1:T(8,128)(2,1)}), bf16[192,5120]{0,1:T(8,128)(2,1)}) %all-gather.11.cloned.1.call-update) | async-done | bytes 1966096 | tf_op jit(solution)/shard_map/all_gather | solution.py:71
  740.7 130.1 %all-gather.9.cloned.1.call-done = bf16[5120,192]{1,0:T(8,128)(2,1)} async-done(((bf16[160,192]{1,0:T(8,128)(2,1)}), bf16[5120,192]{1,0:T(8,128)(2,1)}) %all-gather.9.cloned.1.call-update) | async-done | bytes 1966096 | tf_op jit(solution)/shard_map/all_gather | solution.py:65
  870.8 5.2 convolution_convert_fusion
  876.0 0.0 all-reduce.4.cloned.1.call-update
  876.0 0.0 copy-done.5
  876.0 0.1 copy.30
  876.1 0.0 all-to-all-done.1
  876.1 0.2 reshape.79
  876.4 2.0 gather_fusion.1
  878.4 0.1 reshape.81
  878.4 0.2 multiply_reduce_fusion.1
  878.7 161.6 %all-reduce.4.cloned.1.call-done = bf16[48,5120]{1,0:T(8,128)(2,1)} async-done(((bf16[48,5120]{1,0:T(8,128)(2,1)}), bf16[48,5120]{1,0:T(8,128)(2,1)}) %all-reduce.4.cloned.1.call-update) | async-done | bytes 491536 | tf_op jit(solution)/shard_map/psum | solution.py:75
  1040.3 0.0 copy-done.3
  1040.3 0.9 add_convert_fusion
  1041.2 0.0 copy-start.4
  1041.2 27.8 %all-gather.1 = bf16[16,320,48]{1,2,0:T(8,128)(2,1)S(1)} all-gather(bf16[1,320,48]{1,2,0:T(8,128)(2,1)S(1)} %bitcast.44), channel_id=1, replica_groups=mesh['expert'=32,'tensor'=16] {'tensor'}, dimensions={0}, use_global_device_ids=true | all-gather | bytes 522240 | tf_op jit(solution)/shard_map/all_gather | solution.py:78
  1069.0 0.0 copy-done.4
  1069.0 0.1 copy.31
  1069.1 0.3 reshape.111
  1069.5 0.2 multiply_reduce_fusion
  1069.7 0.0 copy-done
  1069.7 2.0 convolution_convert_fusion.2
  (13 shorter events, 0.2 us)
Async XLA Ops:
  7.2 1062.5 %copy-start = (bf16[132,5120]{1,0:T(8,128)(2,1)S(1)}, bf16[132,5120]{1,0:T(8,128)(2,1)}, u32[]{:S(2)}) copy-start(bf16[132,5120]{1,0:T(8,128)(2,1)} %param.21) | copy-start | bytes 4055044
  7.2 480.0 %all-gather.13.cloned.1.call-start = ((), (), s32[]{:S(2)}) async-start(), calls=%async_computation.6 | async-start | bytes 2088960 | tf_op jit(solution)/shard_map/all_gather | solution.py:51
  417.4 8.8 copy-start.2
  426.2 4.8 copy-start.1
  426.2 4.8 copy-start.6
  433.7 181.0 %all-gather.7.cloned.1.call-start = ((), (), s32[]{:S(2)}) async-start(), calls=%async_computation.2 | async-start | bytes 2703360 | tf_op jit(solution)/shard_map/all_gather | solution.py:60
  434.5 306.2 %all-gather.11.cloned.1.call-start = ((), (), s32[]{:S(2)}) async-start(), calls=%async_computation.4 | async-start | bytes 2703360 | tf_op jit(solution)/shard_map/all_gather | solution.py:71
  435.2 435.6 %all-gather.9.cloned.1.call-start = ((), (), s32[]{:S(2)}) async-start(), calls=%async_computation.3 | async-start | bytes 2703360 | tf_op jit(solution)/shard_map/all_gather | solution.py:65
  491.3 384.9 %all-to-all-start.1 = ((bf16[32,18,320]{2,1,0:T(8,128)(2,1)}), bf16[32,18,320]{2,1,0:T(8,128)(2,1)S(1)}, u32[]{:S(2)}, u32[]{:S(2)}) async-start(bf16[32,18,320]{2,1,0:T(8,128)(2,1)} %reshape.78), calls=%async_computation.1 | async-start | bytes 1179648 | tf_op jit(solution)/shard_map/all_to_all | solution.py:54
  503.6 536.8 %all-reduce.4.cloned.1.call-start = ((), (), s32[]{:S(2)}) async-start(), calls=%async_computation.5 | async-start | bytes 983040 | tf_op jit(solution)/shard_map/psum | solution.py:75
  617.0 259.0 %copy-start.5 = (f32[48,6]{0,1:T(8,128)S(1)}, f32[48,6]{0,1:T(8,128)}, u32[]{:S(2)}) copy-start(f32[48,6]{0,1:T(8,128)} %param.13) | copy-start | bytes 3460
  876.0 164.4 %copy-start.3 = (bf16[48,320]{1,0:T(8,128)(2,1)S(1)}, bf16[48,320]{1,0:T(8,128)(2,1)}, u32[]{:S(2)}) copy-start(bf16[48,320]{1,0:T(8,128)(2,1)} %param.11) | copy-start | bytes 92164
  1041.2 27.8 %copy-start.4 = (bf16[48,320]{1,0:T(8,128)(2,1)}, bf16[48,320]{1,0:T(8,128)(2,1)S(1)}, u32[]{:S(2)}) copy-start(bf16[48,320]{1,0:T(8,128)(2,1)S(1)} %add_convert_fusion) | copy-start | bytes 92164
Sparse Core Ops, SparseCore 0:
  433.8 53.3 all-gather.12
  489.3 125.3 all-gather.6
  616.8 123.8 all-gather.10
  742.6 128.1 all-gather.8
  876.1 164.1 all-reduce.3
where the time goes:
time: 1080 us
  waiting for transfers between devices  580 us (54%)
  blocking collectives  416 us (39%)
  local copies, waits for them, and re-layouts  32.6 us (3%)
  matrix products  19.7 us (2%)
  between operations  14 us (1%)
  starting transfers between devices  12.7 us (1%)
    all_to_all x1, blocking collectives, per_device(): lax.all_to_all(outgoing, 'expert', split_axis=0, concat_axis=0, tiled=True)  359 us
    psum x1, waiting for transfers between devices, per_device(): lax.psum(shared_terms.astype(jnp.bfloat16), 'tensor').astype(jnp.float32)  162 us
    all_gather x1, waiting for transfers between devices, per_device(): lax.all_gather(shared_up, 'expert', axis=0, tiled=True)  130 us
    all_gather x1, waiting for transfers between devices, per_device(): lax.all_gather(shared_down, 'expert', axis=1, tiled=True)  124 us
    all_gather x1, waiting for transfers between devices, per_device(): lax.all_gather(shared_gate, 'expert', axis=0, tiled=True)  111 us
    all_gather x1, waiting for transfers between devices, per_device(): hidden_all = lax.all_gather(hidden, 'tensor', axis=1, tiled=True)  51.4 us
    all_gather x1, blocking collectives, per_device(): features = lax.all_gather(tokens, 'tensor', axis=1, tiled=True)  29.4 us
    all_gather x1, blocking collectives, per_device(): stream_all = lax.all_gather(stream, 'tensor', axis=1, tiled=True)  27.8 us
  transfers between devices with their start and end apart: 6, of which 5 were waited for; matrix products, arithmetic and copies ran while one was open for 1% of the time, Pallas kernels for 0%

commit v1 on v0

--- a/solution.py
+++ b/solution.py
@@ -57,7 +57,10 @@
     routed = jnp.sum(picked * route_weights[:, :, None], axis=1)
     gate_sum = jnp.dot(
         features,
-        lax.all_gather(shared_gate, "expert", axis=0, tiled=True),
+        jnp.concatenate(
+            lax.all_to_all(jnp.stack([shared_gate] * lax.axis_size("expert")), "expert", 0, 0),
+            axis=0,
+        ),
         preferred_element_type=jnp.float32,
     )
     up_sum = jnp.dot(

time: 1080 us -> 974 us (0.902)
  waiting for transfers between devices: 580 us -> 467 us
    all_gather x1 -> x0, waiting for transfers between devices: 111 us -> none  [per_device(): lax.all_gather(shared_gate, 'expert', axis=0, tiled=True)]
    all_to_all x0 -> x1, waiting for transfers between devices: none -> 73 us  [per_device(): lax.all_to_all(jnp.stack([shared_gate] * lax.axis_size('expert')), 'exper...]
    all_gather x1, waiting for transfers between devices: 130 us -> 65.8 us  [per_device(): lax.all_gather(shared_up, 'expert', axis=0, tiled=True)]
  transfers between devices with their start and end apart: 6 -> 6, of which waited for: 5 -> 5; matrix products, arithmetic and copies ran while one was open for 1% -> 2% of each run, Pallas kernels for 0% -> 0%
where the time goes in v1:
time: 974 us; the launch traced here: 973 us
  waiting for transfers between devices  467 us (48%)
  blocking collectives  416 us (43%)
  local copies, waits for them, and re-layouts  34.4 us (4%)
  matrix products  19.7 us (2%)
  starting transfers between devices  18.1 us (2%)
  between operations  14 us (1%)
    all_to_all x1, blocking collectives, per_device(): lax.all_to_all(outgoing, 'expert', split_axis=0, concat_axis=0, tiled=True)  359 us
    psum x1, waiting for transfers between devices, per_device(): lax.psum(shared_terms.astype(jnp.bfloat16), 'tensor').astype(jnp.float32)  162 us
    all_gather x1, waiting for transfers between devices, per_device(): lax.all_gather(shared_down, 'expert', axis=1, tiled=True)  121 us
    all_to_all x1, waiting for transfers between devices, per_device(): lax.all_to_all(jnp.stack([shared_gate] * lax.axis_size('expert')), 'exper...  73 us
    all_gather x1, waiting for transfers between devices, per_device(): lax.all_gather(shared_up, 'expert', axis=0, tiled=True)  65.8 us
    all_gather x1, waiting for transfers between devices, per_device(): hidden_all = lax.all_gather(hidden, 'tensor', axis=1, tiled=True)  44.8 us
    all_gather x1, blocking collectives, per_device(): features = lax.all_gather(tokens, 'tensor', axis=1, tiled=True)  29.4 us
    all_gather x1, blocking collectives, per_device(): stream_all = lax.all_gather(stream, 'tensor', axis=1, tiled=True)  27.8 us
  transfers between devices with their start and end apart: 6, of which 5 were waited for; matrix products, arithmetic and copies ran while one was open for 2% of the time, Pallas kernels for 0%

profile of v1, /device:TPU:1, one launch (start us, length us, event | category | flops | bytes accessed | tf_op | source)
XLA Modules:
  0.0 973.3 jit_solution(8107992231485424440)
XLA Ops:
  7.2 0.0 copy-start
  7.2 0.0 all-gather.10.cloned.1.call-start
  7.2 0.9 copy.26
  8.1 0.7 broadcast_multiply_fusion
  8.8 0.1 eq.22
  8.9 0.9 reduce-window.6
  9.8 0.2 slice_reduce_fusion
  10.1 0.1 bitcast_bitcast_fusion
  10.2 0.1 copy.25
  10.3 0.1 mul.68
  10.4 0.1 reshape.108
  10.6 2.9 scatter_custom_fusion
  13.5 29.4 %all-gather = bf16[16,320,48]{1,2,0:T(8,128)(2,1)S(1)} all-gather(bf16[1,320,48]{1,2,0:T(8,128)(2,1)} %bitcast.44), channel_id=1, replica_groups=mesh['expert'=32,'tensor'=16] {'tensor'}, dimensions={0}, use_global_device_ids=true | all-gather | bytes 522240 | tf_op jit(solution)/shard_map/all_gather | solution.py:35
  43.0 0.1 copy.24
  43.1 0.4 reshape.114
  43.6 6.0 gather_fusion
  49.6 8.5 reshape.82
  58.1 359.3 %all_to_all.15 = bf16[32,18,5120]{2,1,0:T(8,128)(2,1)} all-to-all(bf16[32,18,5120]{2,1,0:T(8,128)(2,1)} %reshape.82), channel_id=1, replica_groups=mesh['expert'=32,'tensor'=16] {'expert'}, dimensions={0} | all-to-all | bytes 11796480 | tf_op jit(solution)/shard_map/all_to_all | solution.py:47
  417.4 8.8 reshape.83
  426.2 0.0 copy-done.2
  426.2 4.8 fusion.4
  431.0 0.0 copy-done.1
  431.0 0.0 copy-done.7
  431.1 0.0 copy-start.5
  431.1 2.7 fusion
  433.7 0.0 all-gather.10.cloned.1.call-update
  433.7 0.0 copy-done.5
  433.8 1.9 stack.2
  435.6 6.5 all-to-all-start
  442.1 0.0 all-gather.6.cloned.1.call-start
  442.1 0.7 all-gather.6.cloned.1.call-update
  442.8 0.0 all-gather.8.cloned.1.call-start
  442.9 0.7 all-gather.8.cloned.1.call-update
  443.6 44.8 %all-gather.10.cloned.1.call-done = bf16[576,1536]{0,1:T(8,128)(2,1)} async-done(((bf16[576,96]{0,1:T(8,128)(2,1)}), bf16[576,1536]{0,1:T(8,128)(2,1)}) %all-gather.10.cloned.1.call-update) | async-done | bytes 1769488 | tf_op jit(solution)/shard_map/all_gather | solution.py:51
  488.4 2.8 convolution_convert_fusion.1
  491.2 0.2 copy.29
  491.4 1.0 reshape.84
  492.4 73.0 %all-to-all-done = bf16[32,160,192]{2,1,0:T(8,128)(2,1)} async-done(((bf16[32,160,192]{2,1,0:T(8,128)(2,1)}), bf16[32,160,192]{2,1,0:T(8,128)(2,1)}, u32[]{:S(2)}, u32[]{:S(2)}) %all-to-all-start) | async-done | bytes 1966112 | tf_op jit(solution)/shard_map/all_to_all | solution.py:61
  565.4 11.3 %all-to-all-start.2 = ((bf16[32,18,320]{2,1,0:T(8,128)(2,1)}), bf16[32,18,320]{2,1,0:T(8,128)(2,1)S(1)}, u32[]{:S(2)}, u32[]{:S(2)}) async-start(bf16[32,18,320]{2,1,0:T(8,128)(2,1)} %reshape.84), calls=%async_computation.2 | async-start | bytes 1179648 | tf_op jit(solution)/shard_map/all_to_all | solution.py:54
  576.7 0.2 all-reduce.4.cloned.1.call-start
  576.9 2.3 fusion.20
  579.3 0.0 copy-start.6
  579.3 65.8 %all-gather.6.cloned.1.call-done = bf16[5120,192]{1,0:T(8,128)(2,1)} async-done(((bf16[160,192]{1,0:T(8,128)(2,1)}), bf16[5120,192]{1,0:T(8,128)(2,1)}) %all-gather.6.cloned.1.call-update) | async-done | bytes 1966096 | tf_op jit(solution)/shard_map/all_gather | solution.py:68
  645.1 120.8 %all-gather.8.cloned.1.call-done = bf16[192,5120]{0,1:T(8,128)(2,1)} async-done(((bf16[192,160]{0,1:T(8,128)(2,1)}), bf16[192,5120]{0,1:T(8,128)(2,1)}) %all-gather.8.cloned.1.call-update) | async-done | bytes 1966096 | tf_op jit(solution)/shard_map/all_gather | solution.py:74
  765.9 5.2 convolution_convert_fusion
  771.1 0.0 all-reduce.4.cloned.1.call-update
  771.1 0.0 copy-done.6
  771.1 0.1 copy.30
  771.2 0.0 all-to-all-done.2
  771.3 0.2 reshape.85
  771.5 2.0 gather_fusion.1
  773.5 0.1 reshape.87
  773.6 0.2 multiply_reduce_fusion.1
  773.8 161.6 %all-reduce.4.cloned.1.call-done = bf16[48,5120]{1,0:T(8,128)(2,1)} async-done(((bf16[48,5120]{1,0:T(8,128)(2,1)}), bf16[48,5120]{1,0:T(8,128)(2,1)}) %all-reduce.4.cloned.1.call-update) | async-done | bytes 491536 | tf_op jit(solution)/shard_map/psum | solution.py:78
  935.5 0.0 copy-done.3
  935.5 0.9 add_convert_fusion
  936.3 0.0 copy-start.4
  936.4 27.8 %all-gather.1 = bf16[16,320,48]{1,2,0:T(8,128)(2,1)S(1)} all-gather(bf16[1,320,48]{1,2,0:T(8,128)(2,1)S(1)} %bitcast.45), channel_id=1, replica_groups=mesh['expert'=32,'tensor'=16] {'tensor'}, dimensions={0}, use_global_device_ids=true | all-gather | bytes 522240 | tf_op jit(solution)/shard_map/all_gather | solution.py:81
  964.1 0.0 copy-done.4
  964.1 0.1 copy.31
  964.3 0.3 reshape.117
  964.6 0.2 multiply_reduce_fusion
  964.8 0.0 copy-done
  964.8 2.0 convolution_convert_fusion.2
  (15 shorter events, 0.2 us)
Async XLA Ops:
  7.2 957.6 %copy-start = (bf16[132,5120]{1,0:T(8,128)(2,1)S(1)}, bf16[132,5120]{1,0:T(8,128)(2,1)}, u32[]{:S(2)}) copy-start(bf16[132,5120]{1,0:T(8,128)(2,1)} %param.21) | copy-start | bytes 4055044
  7.2 481.2 %all-gather.10.cloned.1.call-start = ((), (), s32[]{:S(2)}) async-start(), calls=%async_computation.6 | async-start | bytes 2088960 | tf_op jit(solution)/shard_map/all_gather | solution.py:51
  417.4 8.8 copy-start.2
  426.2 4.8 copy-start.1
  426.2 4.8 copy-start.7
  431.1 2.7 copy-start.5
  435.6 129.8 %all-to-all-start = ((bf16[32,160,192]{2,1,0:T(8,128)(2,1)}), bf16[32,160,192]{2,1,0:T(8,128)(2,1)}, u32[]{:S(2)}, u32[]{:S(2)}) async-start(bf16[32,160,192]{2,1,0:T(8,128)(2,1)} %stack.2), calls=%async_computation | async-start | bytes 5242880 | tf_op jit(solution)/shard_map/all_to_all | solution.py:61
  442.1 203.0 %all-gather.6.cloned.1.call-start = ((), (), s32[]{:S(2)}) async-start(), calls=%async_computation.3 | async-start | bytes 2703360 | tf_op jit(solution)/shard_map/all_gather | solution.py:68
  442.8 323.0 %all-gather.8.cloned.1.call-start = ((), (), s32[]{:S(2)}) async-start(), calls=%async_computation.4 | async-start | bytes 2703360 | tf_op jit(solution)/shard_map/all_gather | solution.py:74
  565.4 205.9 %all-to-all-start.2 = ((bf16[32,18,320]{2,1,0:T(8,128)(2,1)}), bf16[32,18,320]{2,1,0:T(8,128)(2,1)S(1)}, u32[]{:S(2)}, u32[]{:S(2)}) async-start(bf16[32,18,320]{2,1,0:T(8,128)(2,1)} %reshape.84), calls=%async_computation.2 | async-start | bytes 1179648 | tf_op jit(solution)/shard_map/all_to_all | solution.py:54
  576.7 358.7 %all-reduce.4.cloned.1.call-start = ((), (), s32[]{:S(2)}) async-start(), calls=%async_computation.5 | async-start | bytes 983040 | tf_op jit(solution)/shard_map/psum | solution.py:78
  579.3 191.9 %copy-start.6 = (f32[48,6]{0,1:T(8,128)S(1)}, f32[48,6]{0,1:T(8,128)}, u32[]{:S(2)}) copy-start(f32[48,6]{0,1:T(8,128)} %param.13) | copy-start | bytes 3460
  771.1 164.4 %copy-start.3 = (bf16[48,320]{1,0:T(8,128)(2,1)S(1)}, bf16[48,320]{1,0:T(8,128)(2,1)}, u32[]{:S(2)}) copy-start(bf16[48,320]{1,0:T(8,128)(2,1)} %param.11) | copy-start | bytes 92164
  936.3 27.8 %copy-start.4 = (bf16[48,320]{1,0:T(8,128)(2,1)}, bf16[48,320]{1,0:T(8,128)(2,1)S(1)}, u32[]{:S(2)}) copy-start(bf16[48,320]{1,0:T(8,128)(2,1)S(1)} %add_convert_fusion) | copy-start | bytes 92164
Sparse Core Ops, SparseCore 0:
  433.9 54.4 all-gather.9
  490.5 154.5 all-gather.5
  647.2 118.6 all-gather.7
  771.3 164.1 all-reduce.3
